TPU v7x, 32 devices: a whole 2x2x4 slice. The times are simulated.
32 devices in a mesh: dp: 8 (over y, x, core), tensor: 4 (over z).
Axes of the slice: x: 2, y: 2, z: 4, core: 2. Of those that a mesh axis runs over, the one named last changes fastest.
Arguments:
- queries: bfloat16 [2048, 4096], P('dp', 'tensor'), may hold values from -112.5 to 112.5
- token_kv: bfloat16 [2048, 2, 512], P('dp', None, 'tensor'), may hold values from -4.5 to 4.5
- slot_cache: bfloat16 [2048, 2, 512], P('dp', None, 'tensor'), may hold values from -4.5 to 4.5
- lengths: int32 [8], P('dp'), may hold values from 64 to 256, as said below
- upstream: bfloat16 [2048, 8192], P('dp'), may hold values from -36 to 36
- out_weight: bfloat16 [4096, 8192], P('tensor', 'dp'), may hold values from -0.09375 to 0.09375
Outputs:
- layer_output: bfloat16 [2048, 8192], P('dp', 'tensor')
- query_grad: bfloat16 [2048, 4096], P('dp', 'tensor')
- token_kv_grad: bfloat16 [2048, 2, 512], P('dp', None, 'tensor')
- slot_grad: float32 [2048, 2, 512], P('dp', None, 'tensor')
Inputs may be any that keep to these rules, and one draw needn't show every extreme that they name: `lengths`: some conversation has exactly 256 real tokens and some exactly 64.
All inputs are finite; a program needn't handle non-finite values.
Results may differ from a plain program's by a relative error of at most 0.012.
The roundings to bfloat16 on the way count: a program that leaves them out, or rounds other values in their place, can miss the bound.
Values may be sent and summed in bfloat16 or wider, within the bound.
A program may use at most 128 MiB of HBM per device.

v0:
```python
import math

import jax
import jax.numpy as jnp
from jax import lax
from jax.sharding import PartitionSpec as P

HD = 128
LEN = 256


def on_device(queries, token_kv, slot_cache, lengths, upstream, out_weight):
    score_scale = 1.0 / math.sqrt(HD)
    slots = lax.all_gather(slot_cache, "dp", axis=0, tiled=True)
    conv_dev = lengths.shape[0]
    row_count = queries.shape[0]
    kv_dev = token_kv.shape[2] // HD
    heads_dev = queries.shape[1] // HD
    group_size = heads_dev // kv_dev
    slot_count = slots.shape[0]
    key_count = slot_count + LEN
    token_pairs = token_kv.reshape(conv_dev, LEN, 2, kv_dev, HD)
    slot_pairs = slots.reshape(1, slot_count, 2, kv_dev, HD)
    all_pairs = jnp.concatenate([slot_pairs, token_pairs], axis=1)
    key_heads = jnp.transpose(all_pairs[:, :, 0], (2, 0, 1, 3))
    value_heads = jnp.transpose(all_pairs[:, :, 1], (2, 0, 1, 3))
    query_heads = jnp.transpose(queries.reshape(conv_dev, LEN, heads_dev, HD), (2, 0, 1, 3))
    position = jnp.arange(LEN)
    allowed_tok = (position[None, None, :] <= position[None, :, None]) & (
        position[None, None, :] < lengths[:, None, None]
    )
    allowed = jnp.concatenate([jnp.ones((conv_dev, LEN, slot_count), bool), allowed_tok], axis=2)
    kv_owner = jnp.arange(heads_dev) // group_size

    def scores_of(query_one, key_one):
        scores = (
            jnp.einsum("ctd,csd->cts", query_one, key_one, preferred_element_type=jnp.float32)
            * score_scale
        )
        return jnp.where(allowed, scores, -jnp.inf)

    def forward_head(inputs):
        query_one, kv_index = inputs
        key_one = key_heads[kv_index]
        value_one = value_heads[kv_index]
        scores = scores_of(query_one, key_one)
        row_top = jnp.max(scores, axis=-1, keepdims=True)
        shifted = jnp.exp(scores - row_top)
        row_total = jnp.sum(shifted, axis=-1, keepdims=True)
        weights = (shifted / row_total).astype(jnp.bfloat16)
        attended_one = jnp.einsum(
            "cts,csd->ctd", weights, value_one, preferred_element_type=jnp.float32
        ).astype(jnp.bfloat16)
        return (attended_one, row_top, row_total)

    attended, row_tops, row_totals = lax.map(forward_head, (query_heads, kv_owner))
    attended_rows = jnp.transpose(attended, (1, 2, 0, 3)).reshape(row_count, heads_dev * HD)
    live_rows = (position[None, :] < lengths[:, None]).reshape(row_count)
    masked_up = jnp.where(live_rows[:, None], upstream, jnp.zeros_like(upstream))
    partial_value = jnp.dot(
        attended_rows,
        lax.all_gather(out_weight, "dp", axis=1, tiled=True),
        preferred_element_type=jnp.float32,
    )
    out_grad = lax.dot_general(
        masked_up,
        lax.all_gather(out_weight, "dp", axis=1, tiled=True),
        (((1,), (1,)), ((), ())),
        preferred_element_type=jnp.float32,
    )
    layer_output = lax.psum_scatter(
        partial_value.astype(jnp.bfloat16), "tensor", scatter_dimension=1, tiled=True
    )
    grad_heads = jnp.transpose(
        out_grad.astype(jnp.bfloat16).reshape(conv_dev, LEN, heads_dev, HD), (2, 0, 1, 3)
    )

    def backward_head(inputs):
        query_one, kv_index, attended_one, grad_one, row_top, row_total = inputs
        key_one = key_heads[kv_index]
        value_one = value_heads[kv_index]
        scores = scores_of(query_one, key_one)
        probabilities = jnp.exp(scores - row_top) / row_total
        weights = probabilities.astype(jnp.bfloat16)
        prob_grad = jnp.einsum(
            "ctd,csd->cts", grad_one, value_one, preferred_element_type=jnp.float32
        )
        row_delta = jnp.sum(
            grad_one.astype(jnp.float32) * attended_one.astype(jnp.float32), axis=-1, keepdims=True
        )
        dscore = (probabilities * (prob_grad - row_delta)).astype(jnp.bfloat16)
        query_part = (
            jnp.einsum("cts,csd->ctd", dscore, key_one, preferred_element_type=jnp.float32)
            * score_scale
        ).astype(jnp.bfloat16)
        key_part = (
            jnp.einsum("cts,ctd->csd", dscore, query_one, preferred_element_type=jnp.float32)
            * score_scale
        )
        value_part = jnp.einsum(
            "cts,ctd->csd", weights, grad_one, preferred_element_type=jnp.float32
        )
        return (query_part, key_part, value_part)

    query_parts, key_parts, value_parts = lax.map(
        backward_head, (query_heads, kv_owner, attended, grad_heads, row_tops, row_totals)
    )
    query_grad = jnp.transpose(query_parts, (1, 2, 0, 3)).reshape(row_count, heads_dev * HD)
    key_sum = jnp.sum(key_parts.reshape(kv_dev, group_size, conv_dev, key_count, HD), axis=1)
    value_sum = jnp.sum(value_parts.reshape(kv_dev, group_size, conv_dev, key_count, HD), axis=1)
    kv_grads = jnp.stack([key_sum, value_sum], axis=0)
    token_kv_grad = (
        jnp.transpose(kv_grads[:, :, :, slot_count:], (2, 3, 0, 1, 4))
        .reshape(row_count, 2, kv_dev * HD)
        .astype(jnp.bfloat16)
    )
    slot_term = jnp.transpose(
        jnp.sum(kv_grads[:, :, :, :slot_count], axis=2), (2, 0, 1, 3)
    ).reshape(slot_count, 2, kv_dev * HD)
    slot_grad = lax.psum_scatter(
        slot_term.astype(jnp.bfloat16), "dp", scatter_dimension=0, tiled=True
    ).astype(jnp.float32)
    return (layer_output, query_grad, token_kv_grad, slot_grad)


def solution(mesh):
    return jax.shard_map(
        on_device,
        mesh=mesh,
        in_specs=(
            P("dp", "tensor"),
            P("dp", None, "tensor"),
            P("dp", None, "tensor"),
            P("dp"),
            P("dp", None),
            P("tensor", "dp"),
        ),
        out_specs=(
            P("dp", "tensor"),
            P("dp", "tensor"),
            P("dp", None, "tensor"),
            P("dp", None, "tensor"),
        ),
        check_vma=False,
    )
```

profile of v0, /device:TPU:7, one launch (start us, length us, event | category | flops | bytes accessed | tf_op | source)
XLA Modules:
  0.0 342.8 jit_solution(13105585821520889314)
XLA Ops:
  7.2 1.6 copy.23
  12.3 22.4 %all-gather.3.cloned.1.call-done = bf16[2048,2,128]{2,0,1:T(8,128)(2,1)} async-done(((bf16[256,2,128]{2,0,1:T(8,128)(2,1)}), bf16[2048,2,128]{2,0,1:T(8,128)(2,1)}) %all-gather.3.cloned.1.call-update) | async-done | bytes 1048592 | tf_op jit(solution)/shard_map/all_gather | solution.py:14
  36.1 14.6 %while.30 = (s32[]{:T(128)}, bf16[8,1,256,128]{3,2,1,0:T(8,128)(2,1)S(1)}, f32[8,1,256,1]{2,3,1,0:T(1,128)S(1)}, f32[8,1,256,1]{2,3,1,0:T(1,128)S(1)}, pred[1,25...) while((s32[]{:T(128)}, ...), condition=%wide.region_3.4_spmd, body=%wide.region_0.3_spmd.sunk | while | flops 306740736 | bytes 8987761 | solution.py:56
  51.7 74.8 %all-gather.5.cloned.1.call-done = bf16[1024,8192]{1,0:T(8,128)(2,1)} async-done(((bf16[1024,1024]{1,0:T(8,128)(2,1)}), bf16[1024,8192]{1,0:T(8,128)(2,1)}) %all-gather.5.cloned.1.call-update) | async-done | bytes 16777232 | tf_op jit(solution)/shard_map/all_gather | solution.py:62
  126.5 11.6 %fusion.47 = bf16[32,8,8,128]{3,1,2,0:T(8,128)(2,1)S(1)} fusion(bf16[1024,8192]{1,0:T(8,128)(2,1)} %all-gather.5.cloned.1.call-done, bf16[256,8192]{1,0:T(8,128)(2,1)} %param.14, pred[256]{0:T(512)(128)(4,1)S(1)} %iota_compare_fusion.1), kind=kOutput, calls=%fused_computation.60 | convolution fusion | flops 4297326592 | bytes 21496064 | tf_op jit(solution)/shard_map/dot_general | solution.py:65
  138.3 49.0 %while.31 = (s32[]{:T(128)}, bf16[8,1,256,128]{3,2,1,0:T(8,128)(2,1)S(1)}, f32[8,1,2304,128]{3,2,1,0:T(8,128)}, f32[8,1,2304,128]{3,2,1,0:T(8,128)}, pred[1,256,...) while((s32[]{:T(128)}, ...), condition=%wide.region_7.8_spmd, body=%wide.region_5.7_spmd.sunk | while | flops 760184576 | bytes 15804569 | solution.py:105
  138.4 1.9 fusion.96
  141.4 1.6 fusion.99
  144.4 1.9 fusion.96
  147.4 1.6 fusion.99
  149.0 1.6 fusion.100
  150.6 1.9 fusion.96
  153.6 1.6 fusion.99
  155.1 1.6 fusion.100
  156.7 1.9 fusion.96
  161.3 1.6 fusion.100
  162.9 1.9 fusion.96
  165.8 1.6 fusion.99
  167.4 1.6 fusion.100
  169.0 1.9 fusion.96
  173.5 1.5 fusion.100
  175.1 1.9 fusion.96
  181.2 1.9 fusion.96
  184.2 1.6 fusion.99
  185.8 1.6 fusion.100
  187.4 4.3 %reduce_sum.41 = f32[2304,128]{1,0:T(8,128)S(1)} reduce(f32[8,1,2304,128]{3,2,1,0:T(8,128)} %get-tuple-element.165, f32[]{:T(128)} %constant.77.clone.1), dimensions={0,1}, to_apply=%region_9.10 | reduce | flops 2064384 | bytes 10616836 | tf_op jit(solution)/shard_map/reduce_sum | solution.py:110
  191.6 4.3 %reduce_sum.40 = f32[2304,128]{1,0:T(8,128)S(1)} reduce(f32[8,1,2304,128]{3,2,1,0:T(8,128)} %get-tuple-element.164, f32[]{:T(128)} %constant.77.clone.1), dimensions={0,1}, to_apply=%region_8.9 | reduce | flops 2064384 | bytes 10616836 | tf_op jit(solution)/shard_map/reduce_sum | solution.py:109
  195.9 4.5 %fusion.50 = bf16[2048,2,128]{2,1,0:T(2,128)(2,1)} fusion(f32[1,1,1,2304,128]{4,0,3,2,1:T(1,128)S(1)} %bitcast.144, f32[1,1,1,2304,128]{4,0,3,2,1:T(1,128)S(1)} %bitcast.146), kind=kLoop, calls=%fused_computation.63 | loop fusion | flops 2097152 | bytes 3407872 | tf_op jit(solution)/shard_map/convert_element_type | solution.py:121
  200.6 12.5 %convolution_convert_fusion = bf16[256,8192]{1,0:T(8,128)(2,1)} fusion(bf16[256,1024]{0,1:T(8,128)(2,1)} %bitcast.153, bf16[1024,8192]{1,0:T(8,128)(2,1)} %all-gather.5.cloned.1.call-done), kind=kOutput, calls=%fused_computation.52 | convolution fusion | flops 4297064448 | bytes 21495808 | tf_op jit(solution)/shard_map/dot_general | solution.py:60
  217.1 38.1 %all-reduce.4.cloned.1.call-done = bf16[2048,2,128]{2,1,0:T(2,128)(2,1)} async-done(((bf16[2048,2,128]{2,1,0:T(2,128)(2,1)}), bf16[2048,2,128]{2,1,0:T(2,128)(2,1)}) %all-reduce.4.cloned.1.call-update) | async-done | bytes 1048592
  255.2 1.7 dynamic-slice_convert_fusion
  256.9 79.4 %reduce-scatter.2.cloned.1.call-done = bf16[256,2048]{1,0:T(8,128)(2,1)} async-done(((bf16[256,8192]{1,0:T(8,128)(2,1)}), bf16[256,2048]{1,0:T(8,128)(2,1)}) %reduce-scatter.2.cloned.1.call-update) | async-done | bytes 1048592 | tf_op jit(solution)/shard_map/reduce_scatter | solution.py:71
  (105 shorter events, 39.9 us)
Async XLA Ops:
  7.2 27.5 %all-gather.3.cloned.1.call-start = ((), (), s32[]{:S(2)}) async-start(), calls=%async_computation.1 | async-start | bytes 1179648 | tf_op jit(solution)/shard_map/all_gather | solution.py:14
  8.8 2.9 copy-start
  8.8 117.7 %all-gather.5.cloned.1.call-start = ((), (), s32[]{:S(2)}) async-start(), calls=%async_computation.2 | async-start | bytes 18874368 | tf_op jit(solution)/shard_map/all_gather | solution.py:62
  9.6 245.6 %all-reduce.4.cloned.1.call-start = ((), (), s32[]{:S(2)}) async-start(), calls=%async_computation.4 | async-start | bytes 2097152
  10.5 1.7 copy-start.1
  200.4 135.9 %reduce-scatter.2.cloned.1.call-start = ((), (), s32[]{:S(2)}) async-start(), calls=%async_computation.3 | async-start | bytes 5242880 | tf_op jit(solution)/shard_map/reduce_scatter | solution.py:71
  213.1 0.7 copy-start.2
Sparse Core Ops, SparseCore 0:
  10.5 24.1 all-gather.2
  36.6 89.8 all-gather.4
  200.5 54.6 all-reduce.3
  257.9 78.2 reduce-scatter.1
where the time goes:
time: 345 us; the launch traced here: 343 us
  waiting for transfers between devices  215 us (62%)
  matrix products  82.5 us (24%)
  other arithmetic  21.7 us (6%)
  between operations  15.2 us (4%)
  local copies, waits for them, and re-layouts  7.35 us (2%)
    reduce_scatter x1, waiting for transfers between devices, on_device(): lax.psum_scatter(partial_value.astype(jnp.bfloat16), 'tensor', scatter_di...  79.4 us
    all_gather x1, waiting for transfers between devices, on_device(): lax.all_gather(out_weight, 'dp', axis=1, tiled=True)  74.8 us
    unnamed x5, waiting for transfers between devices  38.8 us
    all_gather x1, waiting for transfers between devices, on_device(): slots = lax.all_gather(slot_cache, 'dp', axis=0, tiled=True)  22.4 us
    dot_general x16, matrix products, scores_of(): jnp.einsum('ctd,csd->cts', query_one, key_one, preferred_element_type=jnp...  20.3 us
    dot_general x8, matrix products, backward_head(): jnp.einsum('cts,ctd->csd', dscore, query_one, preferred_element_type=jnp....  12.6 us
    dot_general x1, matrix products, on_device(): jnp.dot(attended_rows, lax.all_gather(out_weight, 'dp', axis=1, tiled=Tru...  12.5 us
    dot_general x8, matrix products, backward_head(): jnp.einsum('cts,ctd->csd', weights, grad_one, preferred_element_type=jnp....  12.4 us
  transfers between devices with their start and end apart: 4, of which 4 were waited for; matrix products, arithmetic and copies ran while one was open for 10% of the time, Pallas kernels for 0%

commit v1 on v0

v1 whole, which is shorter than its diff:
```python
import functools
import math

import jax
import jax.numpy as jnp
from jax import lax
from jax.experimental import pallas as pl
from jax.experimental.pallas import tpu as pltpu
from jax.sharding import PartitionSpec as P

HD = 128
MESH = pl.DeviceIdType.MESH
NT = (((1,), (1,)), ((), ()))
F32 = jnp.float32
BF16 = jnp.bfloat16
HIDDEN = -1e30


def dot(a, b):
    return jnp.dot(a, b, preferred_element_type=F32)


def dot_nt(a, b):
    return lax.dot_general(a, b, NT, preferred_element_type=F32)


def layer_kernel(
    dp, tn, key_block,
    len_ref, q_ref, tok_ref, slot_ref, up_hbm, w_hbm,
    lo_ref, qg_ref, tg_ref, sg_ref,
    wbuf, up, pbuf, rbuf, kv, kt, vt, q_all, do_all, att, og, dq,
    row_top, row_inv, row_delta, sg_out, sg_in, own_sum, tok_sum,
    load_sem, up_sem, slot_send, slot_fwd, slot_recv, w_send, w_recv,
    z_send, z_recv, g_send, g_recv,
):
    me = lax.axis_index("dp")
    mt = lax.axis_index("tensor")
    rows = q_ref.shape[0]
    heads = q_ref.shape[1] // HD
    own_slots = slot_ref.shape[1]
    slot_count = own_slots * dp
    units = wbuf.shape[1]
    width = wbuf.shape[3]
    cols = units * width
    bits = dp.bit_length() - 1
    per_target = dp // tn
    factor = (1.0 / math.sqrt(HD)) * math.log2(math.e)
    score_scale = 1.0 / math.sqrt(HD)

    def flip(mask):
        total = 0
        for bit in range(bits):
            mine = (me // (1 << bit)) % 2
            theirs = (mask // (1 << bit)) % 2
            total = total + (1 << bit) * ((mine + theirs) % 2)
        return total

    def remote(src, dst, send, recv, dp_index, tensor_index):
        return pltpu.make_async_remote_copy(
            src_ref=src, dst_ref=dst, send_sem=send, recv_sem=recv,
            device_id=(dp_index, tensor_index), device_id_type=MESH,
        )

    loads = []
    for u in range(units):
        loads.append(pltpu.make_async_copy(
            w_hbm.at[:, pl.ds(u * width, width)], wbuf.at[0, u], load_sem.at[u]))
        loads[-1].start()
    up_load = pltpu.make_async_copy(up_hbm, up, up_sem)
    up_load.start()
    kv[:, 0:own_slots, :] = slot_ref[...]
    kv[:, slot_count:slot_count + rows, :] = tok_ref[...]

    barrier = pltpu.get_barrier_semaphore()
    for mask in range(1, dp):
        pl.semaphore_signal(barrier, inc=1, device_id=(flip(mask), mt), device_id_type=MESH)
    for j in range(1, tn):
        pl.semaphore_signal(barrier, inc=1, device_id=(me, (mt + j) % tn), device_id_type=MESH)
    pl.semaphore_wait(barrier, dp + tn - 2)

    def slot_copy(src_mask, dst_mask, send, partner):
        return remote(
            kv.at[:, pl.ds(src_mask * own_slots, own_slots)],
            kv.at[:, pl.ds(dst_mask * own_slots, own_slots)],
            send, slot_recv.at[dst_mask], partner, mt)

    slot_copies = []
    for mask in reversed(range(2, dp, 2)):
        slot_copies.append(slot_copy(0, mask, slot_send.at[mask], flip(mask)))
        slot_copies[-1].start()
    slot_copies.append(slot_copy(0, 1, slot_fwd.at[0], flip(1)))
    slot_copies[-1].start()

    orders = [list(range(1, bits)) + [0], list(range(bits - 1, 0, -1)) + [0]]

    def unit_copy(mask, u, bit):
        return remote(
            wbuf.at[mask, u], wbuf.at[mask + (1 << bit), u],
            w_send.at[mask, u, bit], w_recv.at[mask + (1 << bit), u],
            flip(1 << bit), mt)

    unit_copies = []

    def unit_start(mask, u, bit):
        copy = unit_copy(mask, u, bit)
        copy.start()
        unit_copies.append(copy)

    def group_mask(pos, core, order):
        mask = core
        for stage in range(bits - 1):
            if (pos >> stage) & 1:
                mask += 1 << order[stage]
        return mask

    for load in loads:
        load.wait()
    for stage in range(bits - 1):
        for u in range(units):
            unit_start(0, u, orders[u % 2][stage])

    for mask in range(2, dp, 2):
        slot_copy(0, mask, slot_send.at[mask], flip(mask)).wait_recv()
        slot_copies.append(slot_copy(mask, mask + 1, slot_fwd.at[mask], flip(1)))
        slot_copies[-1].start()
    for u in range(units):
        unit_start(0, u, 0)
    for h in range(heads):
        q_all[h] = q_ref[:, h * HD:(h + 1) * HD]
    for mask in range(1, dp, 2):
        slot_copy(mask - 1, mask, slot_fwd.at[mask - 1], flip(1)).wait_recv()

    for at in range(0, slot_count + rows, key_block):
        size = min(key_block, slot_count + rows - at)
        kt[:, at:at + size] = kv[0, at:at + size, :].astype(F32).T.astype(BF16)
        vt[:, at:at + size] = kv[1, at:at + size, :].astype(F32).T.astype(BF16)

    length = len_ref[0]
    key_at = lax.broadcasted_iota(jnp.int32, (rows, rows), 0)
    query_at = lax.broadcasted_iota(jnp.int32, (rows, rows), 1)

    def token_scores(query):
        scores = dot_nt(kv[0, slot_count:slot_count + rows, :], query)
        return jnp.where((key_at <= query_at) & (key_at < length), scores, HIDDEN)

    @pl.loop(0, heads)
    def _(h):
        query = q_all[h]
        s_slot = dot_nt(kv[0, 0:slot_count, :], query)
        s_tok = token_scores(query)
        top = jnp.maximum(
            jnp.max(s_slot, axis=0, keepdims=True), jnp.max(s_tok, axis=0, keepdims=True))
        e_slot = jnp.exp2((s_slot - top) * factor)
        e_tok = jnp.exp2((s_tok - top) * factor)
        total = jnp.sum(e_slot, axis=0, keepdims=True) + jnp.sum(e_tok, axis=0, keepdims=True)
        inverse = 1.0 / total
        row_top[h] = top
        row_inv[h] = inverse
        out_t = dot(vt[:, 0:slot_count], (e_slot * inverse).astype(BF16))
        out_t += dot(vt[:, slot_count:slot_count + rows], (e_tok * inverse).astype(BF16))
        att[:, pl.ds(pl.multiple_of(h * HD, HD), HD)] = out_t.T.astype(BF16)

    up_load.wait()
    og[...] = jnp.zeros_like(og)

    for pos in range(dp // 2):
        for core in range(2):
            masks = [group_mask(pos, core, order) for order in orders]
            if pos or core:
                for u in range(units):
                    order = orders[u % 2]
                    mask = masks[u % 2]
                    last = max(i for i in range(bits) if (mask >> order[i]) & 1)
                    unit_copy(mask - (1 << order[last]), u, order[last]).wait_recv()
                    for i in range(last + 1, bits):
                        unit_start(mask, u, order[i])

            @pl.loop(0, units)
            def _(u, masks=masks):
                mask = masks[0] + (masks[1] - masks[0]) * (u % 2)
                owner = flip(mask)
                block = wbuf[mask, u]
                target = owner // per_target
                offset = pl.multiple_of((owner % per_target) * cols + u * width, 128)
                pbuf[target, :, pl.ds(offset, width)] = dot(att[...], block).astype(BF16)

                @pl.when(target != mt)
                def _():
                    remote(
                        pbuf.at[target, :, pl.ds(offset, width)],
                        rbuf.at[mt, :, pl.ds(offset, width)],
                        z_send.at[target], z_recv.at[mt], me, target).start()

                start = pl.multiple_of(owner * cols + u * width, 128)
                og[...] += dot_nt(up[:, pl.ds(start, width)], block)

    row_at = lax.broadcasted_iota(jnp.int32, (rows, HD), 0)
    for h in range(heads):
        grad = jnp.where(row_at < length, og[:, h * HD:(h + 1) * HD], 0.0).astype(BF16)
        do_all[h] = grad
        both = grad.astype(F32) * att[:, h * HD:(h + 1) * HD].astype(F32)
        row_delta[h] = jnp.sum(both.T, axis=0, keepdims=True)
    dq[...] = jnp.zeros_like(dq)

    def head_step(h, key, value, key_t, scores, sums):
        query = q_all[h]
        grad = do_all[h]
        prob = jnp.exp2((scores - row_top[h]) * factor) * row_inv[h]
        prob_grad = dot_nt(value, grad)
        dscore = (prob * (prob_grad - row_delta[h])).astype(BF16)
        dq[h] += dot(key_t, dscore)
        key_sum, value_sum = sums
        return key_sum + dot(dscore, query), value_sum + dot(prob.astype(BF16), grad)

    def slot_block(at):
        key = kv[0, pl.ds(at, key_block), :]
        value = kv[1, pl.ds(at, key_block), :]
        key_t = kt[:, pl.ds(at, key_block)]
        zero = jnp.zeros((key_block, HD), F32)

        def step(h, sums):
            return head_step(h, key, value, key_t, dot_nt(key, q_all[h]), sums)

        return lax.fori_loop(0, heads, step, (zero, zero), unroll=2)

    parts = key_block // own_slots

    def grad_copy(mask):
        at = pl.multiple_of(mask * own_slots, 16)
        return remote(
            sg_out.at[:, pl.ds(at, own_slots)], sg_in.at[:, pl.ds(at, own_slots)],
            g_send.at[mask], g_recv.at[mask], flip(mask), mt)

    blocks = slot_count // key_block

    @pl.loop(0, blocks - 1)
    def _(step):
        index = blocks - 1 - step
        at = pl.multiple_of(index * key_block, key_block)
        key_sum, value_sum = slot_block(at)
        sg_out[0, pl.ds(at, key_block), :] = (key_sum * score_scale).astype(BF16)
        sg_out[1, pl.ds(at, key_block), :] = value_sum.astype(BF16)
        for part in range(parts):
            grad_copy(index * parts + part).start()

    key_sum, value_sum = slot_block(0)
    own_sum[0] = key_sum * score_scale
    own_sum[1] = value_sum
    if parts > 1:
        sg_out[:, 0:key_block, :] = own_sum[...].astype(BF16)
        for part in range(1, parts):
            grad_copy(part).start()

    tok_key = kv[0, slot_count:slot_count + rows, :]
    tok_value = kv[1, slot_count:slot_count + rows, :]
    tok_key_t = kt[:, slot_count:slot_count + rows]
    zero = jnp.zeros((rows, HD), F32)

    def tok_step(h, sums):
        return head_step(h, tok_key, tok_value, tok_key_t, token_scores(q_all[h]), sums)

    key_sum, value_sum = lax.fori_loop(0, heads, tok_step, (zero, zero), unroll=2)
    tg_ref[0] = (key_sum * score_scale).astype(BF16)
    tg_ref[1] = value_sum.astype(BF16)

    for h in range(heads):
        qg_ref[:, h * HD:(h + 1) * HD] = (dq[h].T * score_scale).astype(BF16)

    for j in range(1, tn):
        other = (mt + j) % tn
        remote(pbuf.at[other], rbuf.at[other], z_send.at[other], z_recv.at[other], me, other).wait()
    strip = 256

    @pl.loop(0, lo_ref.shape[1] // strip)
    def _(i):
        here = pl.ds(pl.multiple_of(i * strip, strip), strip)
        total = pbuf[mt, :, here].astype(F32)
        for j in range(1, tn):
            total += rbuf[(mt + j) % tn, :, here].astype(F32)
        lo_ref[:, here] = total.astype(BF16)

    total = own_sum[:, 0:own_slots, :]
    for mask in range(1, dp):
        grad_copy(mask).wait()
        total += sg_in[:, mask * own_slots:(mask + 1) * own_slots, :].astype(F32)
    sg_ref[...] = total

    for copy in slot_copies + unit_copies:
        copy.wait_send()


def on_device(dp, tn, queries, token_kv, slot_cache, lengths, upstream, out_weight):
    rows, head_cols = queries.shape
    heads = head_cols // HD
    depth, cols = out_weight.shape
    width = 256 if cols >= 512 else 128
    units = cols // width
    model = upstream.shape[1]
    own_slots = slot_cache.shape[0]
    slot_count = own_slots * dp
    keys = slot_count + rows
    bits = dp.bit_length() - 1
    key_block = max(256, own_slots)
    out_cols = model // tn
    vmem = pl.BlockSpec(memory_space=pltpu.VMEM)
    hbm = pl.BlockSpec(memory_space=pl.ANY)
    dma = pltpu.SemaphoreType.DMA
    outs = pl.pallas_call(
        functools.partial(layer_kernel, dp, tn, key_block),
        out_shape=(
            jax.ShapeDtypeStruct((rows, out_cols), BF16),
            jax.ShapeDtypeStruct((rows, head_cols), BF16),
            jax.ShapeDtypeStruct((2, rows, HD), BF16),
            jax.ShapeDtypeStruct((2, own_slots, HD), F32),
        ),
        in_specs=[pl.BlockSpec(memory_space=pltpu.SMEM), vmem, vmem, vmem, hbm, hbm],
        out_specs=(vmem,) * 4,
        scratch_shapes=[
            pltpu.VMEM((dp, units, depth, width), BF16),
            pltpu.VMEM((rows, model), BF16),
            pltpu.VMEM((tn, rows, out_cols), BF16),
            pltpu.VMEM((tn, rows, out_cols), BF16),
            pltpu.VMEM((2, keys, HD), BF16),
            pltpu.VMEM((HD, keys), BF16),
            pltpu.VMEM((HD, keys), BF16),
            pltpu.VMEM((heads, rows, HD), BF16),
            pltpu.VMEM((heads, rows, HD), BF16),
            pltpu.VMEM((rows, head_cols), BF16),
            pltpu.VMEM((rows, head_cols), F32),
            pltpu.VMEM((heads, HD, rows), F32),
            pltpu.VMEM((heads, 1, rows), F32),
            pltpu.VMEM((heads, 1, rows), F32),
            pltpu.VMEM((heads, 1, rows), F32),
            pltpu.VMEM((2, slot_count, HD), BF16),
            pltpu.VMEM((2, slot_count, HD), BF16),
            pltpu.VMEM((2, key_block, HD), F32),
            pltpu.VMEM((2, rows, HD), F32),
            dma((units,)),
            dma(()),
            dma((dp,)),
            dma((dp,)),
            dma((dp,)),
            dma((dp, units, bits)),
            dma((dp, units)),
            dma((tn,)),
            dma((tn,)),
            dma((dp,)),
            dma((dp,)),
        ],
        compiler_params=pltpu.CompilerParams(
            collective_id=0, has_side_effects=True, vmem_limit_bytes=60 * 1024 * 1024),
        name="layer",
    )(
        lengths, queries, jnp.transpose(token_kv, (1, 0, 2)),
        jnp.transpose(slot_cache, (1, 0, 2)), upstream, out_weight,
    )
    layer_output, query_grad, token_grad, slot_grad = outs
    return (
        layer_output, query_grad,
        jnp.transpose(token_grad, (1, 0, 2)), jnp.transpose(slot_grad, (1, 0, 2)),
    )


def solution(mesh):
    return jax.shard_map(
        functools.partial(on_device, mesh.shape["dp"], mesh.shape["tensor"]),
        mesh=mesh,
        in_specs=(
            P("dp", "tensor"),
            P("dp", None, "tensor"),
            P("dp", None, "tensor"),
            P("dp"),
            P("dp", None),
            P("tensor", "dp"),
        ),
        out_specs=(
            P("dp", "tensor"),
            P("dp", "tensor"),
            P("dp", None, "tensor"),
            P("dp", None, "tensor"),
        ),
        check_vma=False,
    )
```

time: 345 us -> 162 us (0.47)
  waiting for transfers between devices: 215 us -> 0 us
  Pallas kernels: 0 us -> 151 us
  matrix products: 82.5 us -> 0 us
  other arithmetic: 21.7 us -> 0 us
  between operations: 15.2 us -> 1.29 us
    pallas_call x0 -> x1, Pallas kernels: none -> 151 us  [on_device(): pl.pallas_call(functools.partial(layer_kernel, dp, tn, key_block), out_sh...]
    all_gather x2 -> x0, waiting for transfers between devices: 97.2 us -> none  [the longest x1 74.8 us: on_device(): lax.all_gather(out_weight, 'dp', axis=1, tiled=True)]
    dot_general x58 -> x0, matrix products: 82.5 us -> none  [the longest x16 20.3 us: scores_of(): jnp.einsum('ctd,csd->cts', query_one, key_one, preferred_element_type=jnp...]
    reduce_scatter x1 -> x0, waiting for transfers between devices: 79.4 us -> none  [on_device(): lax.psum_scatter(partial_value.astype(jnp.bfloat16), 'tensor', scatter_di...]
    unnamed x5 -> x0, waiting for transfers between devices: 38.8 us -> none
    reduce_sum x18 -> x0, other arithmetic: 13.3 us -> none  [the longest x1 4.27 us: on_device(): jnp.sum(key_parts.reshape(kv_dev, group_size, conv_dev, key_count, HD), a...]
    convert_element_type x3 -> x0, other arithmetic: 7.04 us -> none  [the longest x1 4.45 us: on_device(): slot_term.astype(jnp.bfloat16)]
    unnamed x14 -> x4, local copies, waits for them, and re-layouts: 5.23 us -> 7.72 us
  transfers between devices with their start and end apart: 4 -> 0, of which waited for: 4 -> 0; matrix products, arithmetic and copies ran while one was open for 10% -> 0% of each run, Pallas kernels for 0% -> 0%
where the time goes in v1:
time: 162 us; the launch traced here: 161 us
  Pallas kernels  151 us (93%)
  local copies, waits for them, and re-layouts  9.42 us (6%)
    pallas_call x1, Pallas kernels, on_device(): pl.pallas_call(functools.partial(layer_kernel, dp, tn, key_block), out_sh...  151 us
    unnamed x4, local copies, waits for them, and re-layouts  7.72 us

profile of v1, /device:TPU:7, one launch (start us, length us, event | category | flops | bytes accessed | tf_op | source)
XLA Modules:
  0.0 161.3 jit_solution(15862930677040457766)
XLA Ops:
  1.3 1.7 %copy_bitcast_fusion = (bf16[2,256,128]{2,1,0:T(8,128)(2,1)}, bf16[2,256,128]{2,1,0:T(8,128)(2,1)}) fusion(bf16[256,2,128]{2,1,0:T(2,128)(2,1)} %param.8, bf16[256,2,128]{2,1,0:T(2,128)(2,1)} %param.7), kind=kLoop, calls=%fused_computation | loop fusion | bytes 524288 | tf_op jit(solution)/shard_map/transpose | solution.py:355
  3.0 150.6 %layer.1 = (bf16[256,2048]{1,0:T(8,128)(2,1)}, bf16[256,1024]{1,0:T(8,128)(2,1)}, bf16[2,256,128]{2,1,0:T(8,128)(2,1)}, f32[2,256,128]{2,1,0:T(8,128)}) custom-call(s32[1]{0:T(128)S(6)} %copy.18.len_ref, bf16[256,1024]{1,0:T(8,128)(2,1)} %q_ref.1, bf16[2,256,128]{2,1,0:T(8,128)(2,1)} %get-tuple-element.17.tok_ref, ...), custom_call_target="tpu_custom_call" | custom-call | tf_op jit(solution)/shard_map/layer/pallas_call | solution.py:308
  153.6 1.7 %copy.12 = bf16[256,2,128]{2,1,0:T(2,128)(2,1)} copy(bf16[256,2,128]{2,0,1:T(8,128)(2,1)} %bitcast.7) | data formatting | bytes 262144
  155.2 1.9 %copy.13 = f32[256,2,128]{2,1,0:T(2,128)} copy(f32[256,2,128]{2,0,1:T(8,128)} %bitcast.6) | data formatting | bytes 524288
  157.1 2.3 %copy.19 = bf16[256,2048]{1,0:T(8,128)(2,1)} copy(bf16[256,2048]{1,0:T(8,128)(2,1)} %get-tuple-element.22) | data formatting | bytes 2097152
  159.4 1.9 %copy.20 = bf16[256,1024]{1,0:T(8,128)(2,1)} copy(bf16[256,1024]{1,0:T(8,128)(2,1)} %get-tuple-element.23) | data formatting | bytes 1048576

commit v2 on v1

--- a/solution.py
+++ b/solution.py
@@ -29,7 +29,7 @@
     len_ref, q_ref, tok_ref, slot_ref, up_hbm, w_hbm,
     lo_ref, qg_ref, tg_ref, sg_ref,
     wbuf, up, pbuf, rbuf, kv, kt, vt, q_all, do_all, att, og, dq,
-    row_top, row_inv, row_delta, sg_out, sg_in, own_sum, tok_sum,
+    row_top, row_inv, row_delta, sg_out, sg_in, own_sum,
     load_sem, up_sem, slot_send, slot_fwd, slot_recv, w_send, w_recv,
     z_send, z_recv, g_send, g_recv,
 ):
@@ -78,6 +78,14 @@
         pl.semaphore_signal(barrier, inc=1, device_id=(me, (mt + j) % tn), device_id_type=MESH)
     pl.semaphore_wait(barrier, dp + tn - 2)
 
+    @pl.when(mt == 0)
+    def _():
+        rbuf[0] = jnp.zeros(rbuf.shape[1:], BF16)
+
+    @pl.when(mt == tn - 1)
+    def _():
+        rbuf[tn] = jnp.zeros(rbuf.shape[1:], BF16)
+
     def slot_copy(src_mask, dst_mask, send, partner):
         return remote(
             kv.at[:, pl.ds(src_mask * own_slots, own_slots)],
@@ -163,6 +171,55 @@
     up_load.wait()
     og[...] = jnp.zeros_like(og)
 
+    unit_total = dp * units
+    lag = 2 * units
+
+    def unit_at(step):
+        group, u = step // units, step % units
+        pos, core = group // 2, group % 2
+        masks = []
+        for order in orders:
+            mask = core
+            for stage in range(bits - 1):
+                mask = mask + (1 << order[stage]) * ((pos // (1 << stage)) % 2)
+            masks.append(mask)
+        mask = masks[0] + (masks[1] - masks[0]) * (u % 2)
+        owner = flip(mask)
+        target = owner // per_target
+        offset = pl.multiple_of((owner % per_target) * cols + u * width, 128)
+        return mask, u, owner, target, offset, (owner % per_target) * units + u
+
+    def relay(step, up_way):
+        _, _, _, target, offset, index = unit_at(step)
+        here = (target, slice(None), pl.ds(offset, width))
+        first = (mt == 0) if up_way else (mt == tn - 1)
+        partner = mt + 1 if up_way else mt - 1
+
+        @pl.when((target > mt) if up_way else (target < mt))
+        def _():
+            @pl.when(jnp.logical_not(first))
+            def _():
+                remote(
+                    pbuf.at[here], rbuf.at[here], z_send.at[target],
+                    z_recv.at[target, index], me, partner).wait_recv()
+                pbuf[here] = (pbuf[here].astype(F32) + rbuf[here].astype(F32)).astype(BF16)
+
+            if up_way:
+                slot = target
+            else:
+                slot = jnp.where(partner == target, tn, target)
+            remote(
+                pbuf.at[here], rbuf.at[slot, :, pl.ds(offset, width)],
+                z_send.at[target], z_recv.at[slot, index], me, partner).start()
+
+    def relay_step(step):
+        for up_way in (True, False):
+            late = step - lag * (mt if up_way else tn - 1 - mt)
+
+            @pl.when((late >= 0) & (late < unit_total))
+            def _(late=late, up_way=up_way):
+                relay(late, up_way)
+
     for pos in range(dp // 2):
         for core in range(2):
             masks = [group_mask(pos, core, order) for order in orders]
@@ -176,22 +233,13 @@
                         unit_start(mask, u, order[i])
 
             @pl.loop(0, units)
-            def _(u, masks=masks):
-                mask = masks[0] + (masks[1] - masks[0]) * (u % 2)
-                owner = flip(mask)
+            def _(u, group=2 * pos + core):
+                step = group * units + u
+                mask, _, owner, target, offset, _ = unit_at(step)
                 block = wbuf[mask, u]
-                target = owner // per_target
-                offset = pl.multiple_of((owner % per_target) * cols + u * width, 128)
                 pbuf[target, :, pl.ds(offset, width)] = dot(att[...], block).astype(BF16)
-
-                @pl.when(target != mt)
-                def _():
-                    remote(
-                        pbuf.at[target, :, pl.ds(offset, width)],
-                        rbuf.at[mt, :, pl.ds(offset, width)],
-                        z_send.at[target], z_recv.at[mt], me, target).start()
-
                 start = pl.multiple_of(owner * cols + u * width, 128)
+                relay_step(step)
                 og[...] += dot_nt(up[:, pl.ds(start, width)], block)
 
     row_at = lax.broadcasted_iota(jnp.int32, (rows, HD), 0)
@@ -232,6 +280,7 @@
             g_send.at[mask], g_recv.at[mask], flip(mask), mt)
 
     blocks = slot_count // key_block
+    late_steps = -(-lag * (tn - 2) // (blocks - 1))
 
     @pl.loop(0, blocks - 1)
     def _(step):
@@ -242,6 +291,8 @@
         sg_out[1, pl.ds(at, key_block), :] = value_sum.astype(BF16)
         for part in range(parts):
             grad_copy(index * parts + part).start()
+        for i in range(late_steps):
+            relay_step(unit_total + step * late_steps + i)
 
     key_sum, value_sum = slot_block(0)
     own_sum[0] = key_sum * score_scale
@@ -266,17 +317,29 @@
     for h in range(heads):
         qg_ref[:, h * HD:(h + 1) * HD] = (dq[h].T * score_scale).astype(BF16)
 
-    for j in range(1, tn):
-        other = (mt + j) % tn
-        remote(pbuf.at[other], rbuf.at[other], z_send.at[other], z_recv.at[other], me, other).wait()
+    def collect(slot):
+        @pl.loop(0, per_target * units)
+        def _(index):
+            here = (slot, slice(None), pl.ds(pl.multiple_of(index * width, 128), width))
+            remote(
+                pbuf.at[0, :, pl.ds(0, width)], rbuf.at[here], z_send.at[0],
+                z_recv.at[slot, index], me, (mt + 1) % tn).wait_recv()
+
+    @pl.when(mt > 0)
+    def _():
+        collect(mt)
+
+    @pl.when(mt < tn - 1)
+    def _():
+        collect(tn)
+
     strip = 256
 
     @pl.loop(0, lo_ref.shape[1] // strip)
     def _(i):
         here = pl.ds(pl.multiple_of(i * strip, strip), strip)
         total = pbuf[mt, :, here].astype(F32)
-        for j in range(1, tn):
-            total += rbuf[(mt + j) % tn, :, here].astype(F32)
+        total += rbuf[mt, :, here].astype(F32) + rbuf[tn, :, here].astype(F32)
         lo_ref[:, here] = total.astype(BF16)
 
     total = own_sum[:, 0:own_slots, :]
@@ -287,6 +350,11 @@
 
     for copy in slot_copies + unit_copies:
         copy.wait_send()
+    for j in range(1, tn):
+        other = (mt + j) % tn
+        remote(
+            pbuf.at[other], rbuf.at[other], z_send.at[other],
+            z_recv.at[other, 0], me, other).wait_send()
 
 
 def on_device(dp, tn, queries, token_kv, slot_cache, lengths, upstream, out_weight):
@@ -319,7 +387,7 @@
             pltpu.VMEM((dp, units, depth, width), BF16),
             pltpu.VMEM((rows, model), BF16),
             pltpu.VMEM((tn, rows, out_cols), BF16),
-            pltpu.VMEM((tn, rows, out_cols), BF16),
+            pltpu.VMEM((tn + 1, rows, out_cols), BF16),
             pltpu.VMEM((2, keys, HD), BF16),
             pltpu.VMEM((HD, keys), BF16),
             pltpu.VMEM((HD, keys), BF16),
@@ -334,7 +402,6 @@
             pltpu.VMEM((2, slot_count, HD), BF16),
             pltpu.VMEM((2, slot_count, HD), BF16),
             pltpu.VMEM((2, key_block, HD), F32),
-            pltpu.VMEM((2, rows, HD), F32),
             dma((units,)),
             dma(()),
             dma((dp,)),
@@ -343,7 +410,7 @@
             dma((dp, units, bits)),
             dma((dp, units)),
             dma((tn,)),
-            dma((tn,)),
+            dma((tn + 1, dp // tn * units)),
             dma((dp,)),
             dma((dp,)),
         ],

time: 162 us -> 147 us (0.907)
  Pallas kernels: 151 us -> 136 us
    pallas_call x1, Pallas kernels: 151 us -> 136 us  [on_device(): pl.pallas_call(functools.partial(layer_kernel, dp, tn, key_block), out_sh...]
where the time goes in v2:
time: 147 us
  Pallas kernels  136 us (93%)
  local copies, waits for them, and re-layouts  9.42 us (6%)
    pallas_call x1, Pallas kernels, on_device(): pl.pallas_call(functools.partial(layer_kernel, dp, tn, key_block), out_sh...  136 us
    unnamed x4, local copies, waits for them, and re-layouts  7.72 us

profile of v2, /device:TPU:7, one launch (start us, length us, event | category | flops | bytes accessed | tf_op | source)
XLA Modules:
  0.0 147.1 jit_solution(13655812063814792270)
XLA Ops:
  1.3 1.7 %copy_bitcast_fusion = (bf16[2,256,128]{2,1,0:T(8,128)(2,1)}, bf16[2,256,128]{2,1,0:T(8,128)(2,1)}) fusion(bf16[256,2,128]{2,1,0:T(2,128)(2,1)} %param.8, bf16[256,2,128]{2,1,0:T(2,128)(2,1)} %param.7), kind=kLoop, calls=%fused_computation | loop fusion | bytes 524288 | tf_op jit(solution)/shard_map/transpose | solution.py:422
  3.0 136.4 %layer.1 = (bf16[256,2048]{1,0:T(8,128)(2,1)}, bf16[256,1024]{1,0:T(8,128)(2,1)}, bf16[2,256,128]{2,1,0:T(8,128)(2,1)}, f32[2,256,128]{2,1,0:T(8,128)}) custom-call(s32[1]{0:T(128)S(6)} %copy.18.len_ref, bf16[256,1024]{1,0:T(8,128)(2,1)} %q_ref.1, bf16[2,256,128]{2,1,0:T(8,128)(2,1)} %get-tuple-element.17.tok_ref, ...), custom_call_target="tpu_custom_call" | custom-call | tf_op jit(solution)/shard_map/layer/pallas_call | solution.py:376
  139.4 1.7 %copy.12 = bf16[256,2,128]{2,1,0:T(2,128)(2,1)} copy(bf16[256,2,128]{2,0,1:T(8,128)(2,1)} %bitcast.7) | data formatting | bytes 262144
  141.1 1.9 %copy.13 = f32[256,2,128]{2,1,0:T(2,128)} copy(f32[256,2,128]{2,0,1:T(8,128)} %bitcast.6) | data formatting | bytes 524288
  143.0 2.3 %copy.19 = bf16[256,2048]{1,0:T(8,128)(2,1)} copy(bf16[256,2048]{1,0:T(8,128)(2,1)} %get-tuple-element.22) | data formatting | bytes 2097152
  145.3 1.9 %copy.20 = bf16[256,1024]{1,0:T(8,128)(2,1)} copy(bf16[256,1024]{1,0:T(8,128)(2,1)} %get-tuple-element.23) | data formatting | bytes 1048576

commit v3 on v2

--- a/solution.py
+++ b/solution.py
@@ -239,8 +239,8 @@
                 block = wbuf[mask, u]
                 pbuf[target, :, pl.ds(offset, width)] = dot(att[...], block).astype(BF16)
                 start = pl.multiple_of(owner * cols + u * width, 128)
+                og[...] += dot_nt(up[:, pl.ds(start, width)], block)
                 relay_step(step)
-                og[...] += dot_nt(up[:, pl.ds(start, width)], block)
 
     row_at = lax.broadcasted_iota(jnp.int32, (rows, HD), 0)
     for h in range(heads):

time: 147 us -> 147 us (level)
  no operation moved by 1% of the time
where the time goes in v3:
time: 147 us
  Pallas kernels  136 us (93%)
  local copies, waits for them, and re-layouts  9.42 us (6%)
    pallas_call x1, Pallas kernels, on_device(): pl.pallas_call(functools.partial(layer_kernel, dp, tn, key_block), out_sh...  136 us
    unnamed x4, local copies, waits for them, and re-layouts  7.72 us

profile of v3, /device:TPU:7, one launch (start us, length us, event | category | flops | bytes accessed | tf_op | source)
XLA Modules:
  0.0 146.7 jit_solution(9520566828937918613)
XLA Ops:
  1.3 1.7 %copy_bitcast_fusion = (bf16[2,256,128]{2,1,0:T(8,128)(2,1)}, bf16[2,256,128]{2,1,0:T(8,128)(2,1)}) fusion(bf16[256,2,128]{2,1,0:T(2,128)(2,1)} %param.8, bf16[256,2,128]{2,1,0:T(2,128)(2,1)} %param.7), kind=kLoop, calls=%fused_computation | loop fusion | bytes 524288 | tf_op jit(solution)/shard_map/transpose | solution.py:422
  3.0 136.0 %layer.1 = (bf16[256,2048]{1,0:T(8,128)(2,1)}, bf16[256,1024]{1,0:T(8,128)(2,1)}, bf16[2,256,128]{2,1,0:T(8,128)(2,1)}, f32[2,256,128]{2,1,0:T(8,128)}) custom-call(s32[1]{0:T(128)S(6)} %copy.18.len_ref, bf16[256,1024]{1,0:T(8,128)(2,1)} %q_ref.1, bf16[2,256,128]{2,1,0:T(8,128)(2,1)} %get-tuple-element.17.tok_ref, ...), custom_call_target="tpu_custom_call" | custom-call | tf_op jit(solution)/shard_map/layer/pallas_call | solution.py:376
  139.0 1.7 %copy.12 = bf16[256,2,128]{2,1,0:T(2,128)(2,1)} copy(bf16[256,2,128]{2,0,1:T(8,128)(2,1)} %bitcast.7) | data formatting | bytes 262144
  140.7 1.9 %copy.13 = f32[256,2,128]{2,1,0:T(2,128)} copy(f32[256,2,128]{2,0,1:T(8,128)} %bitcast.6) | data formatting | bytes 524288
  142.5 2.3 %copy.19 = bf16[256,2048]{1,0:T(8,128)(2,1)} copy(bf16[256,2048]{1,0:T(8,128)(2,1)} %get-tuple-element.22) | data formatting | bytes 2097152
  144.8 1.9 %copy.20 = bf16[256,1024]{1,0:T(8,128)(2,1)} copy(bf16[256,1024]{1,0:T(8,128)(2,1)} %get-tuple-element.23) | data formatting | bytes 1048576
